TPU v7x, 512 devices: a whole 4x4x16 slice. The times are simulated.
512 devices in a mesh: inp: 8 (over x, core), out: 8 (over z_hi, y), dep: 8 (over z_lo).
Axes of the slice: x: 4, y: 4, z: 16 (z_hi: 2, z_lo: 8; z = z_hi * 8 + z_lo), core: 2. Of those that a mesh axis runs over, the one named last changes fastest.
Arguments:
- inputs: bfloat16 [1024, 4096], P('dep', 'inp'), may hold values from -6 to 6
- out_grad: bfloat16 [1024, 4096], P('dep', 'inp'), may hold values from -6 to 6
- gate_weight: bfloat16 [14336, 4096], P(('out', 'dep'), 'inp'), may hold values from -0.09375 to 0.09375
- up_weight: bfloat16 [14336, 4096], P(('out', 'dep'), 'inp'), may hold values from -0.09375 to 0.09375
- down_weight: bfloat16 [14336, 4096], P(('out', 'dep'), 'inp'), may hold values from -0.046875 to 0.046875
Outputs:
- input_grad: bfloat16 [1024, 4096], P(('dep', 'out'), 'inp')
- gate_grad: bfloat16 [14336, 4096], P(('out', 'dep'), 'inp')
- up_grad: bfloat16 [14336, 4096], P(('out', 'dep'), 'inp')
- down_grad: bfloat16 [14336, 4096], P(('out', 'dep'), 'inp')
All inputs are finite; a program needn't handle non-finite values.
Results may differ from a plain program's by a relative error of at most 0.005.
Values may be sent and summed in bfloat16 or wider, within the bound.
A program may use at most 64 MiB of HBM per device.

v0:
```python
import jax
import jax.numpy as jnp
from jax import lax
from jax.sharding import PartitionSpec as P


def elementwise(gate, up, hidden_grad):
    sig = jax.nn.sigmoid(gate)
    hidden = (gate * sig * up).astype(jnp.bfloat16)
    gate_delta = (hidden_grad * up * sig * (1.0 + gate * (1.0 - sig))).astype(jnp.bfloat16)
    up_delta = (hidden_grad * gate * sig).astype(jnp.bfloat16)
    return (hidden, gate_delta, up_delta)


def body(inputs, out_grad, gate_weight, up_weight, down_weight):
    all_inputs, all_grads = (
        lax.all_gather(inputs, "dep", axis=0, tiled=True),
        lax.all_gather(out_grad, "dep", axis=0, tiled=True),
    )
    gate_full, up_full, down_full = (
        lax.all_gather(gate_weight, "dep", axis=0, tiled=True),
        lax.all_gather(up_weight, "dep", axis=0, tiled=True),
        lax.all_gather(down_weight, "dep", axis=0, tiled=True),
    )
    gate_part = jnp.einsum("tr,cr->tc", inputs, gate_full, preferred_element_type=jnp.float32)
    up_part = jnp.einsum("tr,cr->tc", inputs, up_full, preferred_element_type=jnp.float32)
    grad_part = jnp.einsum("tr,cr->tc", out_grad, down_full, preferred_element_type=jnp.float32)
    gate, up, hidden_grad = lax.psum((gate_part, up_part, grad_part), "inp")
    hidden, gate_delta, up_delta = elementwise(gate, up, hidden_grad)
    hidden_cols, gate_cols, up_cols = (
        lax.all_to_all(hidden, "dep", split_axis=1, concat_axis=0, tiled=True),
        lax.all_to_all(gate_delta, "dep", split_axis=1, concat_axis=0, tiled=True),
        lax.all_to_all(up_delta, "dep", split_axis=1, concat_axis=0, tiled=True),
    )
    total = jnp.dot(gate_delta, gate_full, preferred_element_type=jnp.float32)
    input_grad = lax.psum_scatter(
        total + jnp.dot(up_delta, up_full, preferred_element_type=jnp.float32),
        "out",
        scatter_dimension=0,
        tiled=True,
    )
    gate_grad = jnp.einsum(
        "tc,tr->cr", gate_cols, all_inputs, preferred_element_type=jnp.float32
    ).astype(jnp.bfloat16)
    up_grad = jnp.einsum(
        "tc,tr->cr", up_cols, all_inputs, preferred_element_type=jnp.float32
    ).astype(jnp.bfloat16)
    down_grad = jnp.einsum(
        "tc,tr->cr", hidden_cols, all_grads, preferred_element_type=jnp.float32
    ).astype(jnp.bfloat16)
    return (input_grad.astype(jnp.bfloat16), gate_grad, up_grad, down_grad)


def solution(mesh):
    return jax.shard_map(
        body,
        mesh=mesh,
        in_specs=(
            P("dep", "inp"),
            P("dep", "inp"),
            P(("out", "dep"), "inp"),
            P(("out", "dep"), "inp"),
            P(("out", "dep"), "inp"),
        ),
        out_specs=(
            P(("dep", "out"), "inp"),
            P(("out", "dep"), "inp"),
            P(("out", "dep"), "inp"),
            P(("out", "dep"), "inp"),
        ),
        check_vma=False,
    )
```

profile of v0, /device:TPU:1, one launch (start us, length us, event | category | flops | bytes accessed | tf_op | source)
XLA Modules:
  0.0 565.0 jit_solution(9668017929241101512)
XLA Ops:
  7.2 0.0 copy-start.2
  7.2 0.0 all-gather.8.cloned.1.call-start
  7.2 0.7 all-gather.8.cloned.1.call-update
  7.9 0.0 all-gather.10.cloned.1.call-start
  8.0 0.7 all-gather.10.cloned.1.call-update
  8.7 0.0 all-gather.6.cloned.1.call-start
  8.7 0.7 all-gather.6.cloned.1.call-update
  9.4 0.0 all-reduce.3.cloned.1.call-start
  9.4 70.7 %all-gather.8.cloned.1.call-done = bf16[1792,512]{1,0:T(8,128)(2,1)} async-done(((bf16[224,512]{1,0:T(8,128)(2,1)}), bf16[1792,512]{1,0:T(8,128)(2,1)}) %all-gather.8.cloned.1.call-update) | async-done | bytes 1835024 | tf_op jit(solution)/shard_map/all_gather | solution.py:22
  80.1 3.3 fusion.7
  83.4 0.0 copy-start.3
  83.4 64.4 %all-gather.10.cloned.1.call-done = bf16[1792,512]{1,0:T(8,128)(2,1)} async-done(((bf16[224,512]{1,0:T(8,128)(2,1)}), bf16[1792,512]{1,0:T(8,128)(2,1)}) %all-gather.10.cloned.1.call-update) | async-done | bytes 1835024 | tf_op jit(solution)/shard_map/all_gather | solution.py:21
  147.9 0.0 copy-done.2
  147.9 3.2 fusion.8
  151.0 64.6 %all-gather.6.cloned.1.call-done = bf16[1792,512]{1,0:T(8,128)(2,1)} async-done(((bf16[224,512]{1,0:T(8,128)(2,1)}), bf16[1792,512]{1,0:T(8,128)(2,1)}) %all-gather.6.cloned.1.call-update) | async-done | bytes 1835024 | tf_op jit(solution)/shard_map/all_gather | solution.py:23
  215.6 0.0 copy-done.3
  215.6 3.1 fusion.6
  218.8 0.0 all-reduce.3.cloned.1.call-update
  218.8 82.7 %all-reduce.3.cloned.1.call-done = (f32[128,1792]{1,0:T(8,128)}, f32[128,1792]{1,0:T(8,128)}, f32[128,1792]{1,0:T(8,128)}) async-done(((f32[128,1792]{1,0:T(8,128)}, f32[128,1792]{1,0:T(8,128)}, f32[128,1792]{1,0:T(8,128)}), (f32[128,1792]{1,0:T(8,128)}, f32[128,1792]{1,0:T(8,128)}, f32[128,1792]{1,0:T(8,128)})) %all-reduce.3.cloned.1.call-update) | async-done | bytes 2752528 | tf_op jit(solution)/shard_map/psum | solution.py:28
  301.5 2.2 multiply_convert_fusion
  303.7 0.0 copy-start
  303.7 1.0 copy.11
  304.7 9.7 %all-to-all-start.1 = ((bf16[128,8,224]{0,2,1:T(8,128)(2,1)}), bf16[128,8,224]{0,2,1:T(8,128)(2,1)}, u32[]{:S(2)}, u32[]{:S(2)}) async-start(bf16[128,8,224]{0,2,1:T(8,128)(2,1)} %bitcast.2), calls=%async_computation.2 | async-start | bytes 917504 | tf_op jit(solution)/shard_map/all_to_all | solution.py:33
  314.4 0.0 reduce-scatter.2.cloned.1.call-start
  314.5 0.0 copy-start.1
  314.5 0.0 copy-done
  314.5 0.4 fusion.9
  314.9 1.1 copy-done.1
  316.0 1.1 convolution_add_fusion
  317.1 0.0 reduce-scatter.2.cloned.1.call-update
  317.1 0.0 all-gather.12.cloned.1.call-start
  317.1 0.5 all-gather.12.cloned.1.call-update
  317.7 1.0 copy.9
  318.6 15.0 %all-to-all-done.1 = bf16[128,8,224]{0,2,1:T(8,128)(2,1)} async-done(((bf16[128,8,224]{0,2,1:T(8,128)(2,1)}), bf16[128,8,224]{0,2,1:T(8,128)(2,1)}, u32[]{:S(2)}, u32[]{:S(2)}) %all-to-all-start.1) | async-done | bytes 458784 | tf_op jit(solution)/shard_map/all_to_all | solution.py:33
  333.6 10.4 %all-to-all-start = ((bf16[128,8,224]{0,2,1:T(8,128)(2,1)}), bf16[128,8,224]{0,2,1:T(8,128)(2,1)S(1)}, u32[]{:S(2)}, u32[]{:S(2)}) async-start(bf16[128,8,224]{0,2,1:T(8,128)(2,1)} %bitcast), calls=%async_computation.1 | async-start | bytes 917504 | tf_op jit(solution)/shard_map/all_to_all | solution.py:32
  344.0 0.0 all-gather.14.cloned.1.call-start
  344.1 0.7 all-gather.14.cloned.1.call-update
  344.8 1.0 copy.13
  345.7 18.6 %all-to-all-done = bf16[128,8,224]{0,2,1:T(8,128)(2,1)S(1)} async-done(((bf16[128,8,224]{0,2,1:T(8,128)(2,1)}), bf16[128,8,224]{0,2,1:T(8,128)(2,1)S(1)}, u32[]{:S(2)}, u32[]{:S(2)}) %all-to-all-start) | async-done | bytes 458784 | tf_op jit(solution)/shard_map/all_to_all | solution.py:32
  364.3 10.9 %all-to-all-start.2 = ((bf16[128,8,224]{0,2,1:T(8,128)(2,1)}), bf16[128,8,224]{0,2,1:T(8,128)(2,1)S(1)}, u32[]{:S(2)}, u32[]{:S(2)}) async-start(bf16[128,8,224]{0,2,1:T(8,128)(2,1)} %bitcast.4), calls=%async_computation.3 | async-start | bytes 917504 | tf_op jit(solution)/shard_map/all_to_all | solution.py:31
  375.2 62.3 %reduce-scatter.2.cloned.1.call-done = f32[16,512]{1,0:T(8,128)} async-done(((f32[128,512]{1,0:T(8,128)}), f32[16,512]{1,0:T(8,128)}) %reduce-scatter.2.cloned.1.call-update) | async-done | bytes 32784 | tf_op jit(solution)/shard_map/reduce_scatter | solution.py:36
  437.5 1.4 convert_element_type.23
  438.8 53.6 %all-gather.12.cloned.1.call-done = bf16[1024,512]{1,0:T(8,128)(2,1)} async-done(((bf16[128,512]{1,0:T(8,128)(2,1)}), bf16[1024,512]{1,0:T(8,128)(2,1)}) %all-gather.12.cloned.1.call-update) | async-done | bytes 1048592 | tf_op jit(solution)/shard_map/all_gather | solution.py:17
  492.5 0.0 copy-start.4
  492.5 2.5 convolution_convert_fusion.1
  495.0 0.0 copy-done.4
  495.0 1.1 convolution_convert_fusion.2
  496.1 59.7 %all-gather.14.cloned.1.call-done = bf16[1024,512]{1,0:T(8,128)(2,1)} async-done(((bf16[128,512]{1,0:T(8,128)(2,1)}), bf16[1024,512]{1,0:T(8,128)(2,1)}) %all-gather.14.cloned.1.call-update) | async-done | bytes 1048592 | tf_op jit(solution)/shard_map/all_gather | solution.py:18
  555.9 0.0 all-to-all-done.2
  555.9 2.3 convolution_convert_fusion
Async XLA Ops:
  7.2 140.7 %copy-start.2 = (bf16[128,512]{1,0:T(8,128)(2,1)S(1)}, bf16[128,512]{1,0:T(8,128)(2,1)}, u32[]{:S(2)}) copy-start(bf16[128,512]{1,0:T(8,128)(2,1)} %param.5) | copy-start | bytes 393220
  7.2 72.9 %all-gather.8.cloned.1.call-start = ((), (), s32[]{:S(2)}) async-start(), calls=%async_computation.5 | async-start | bytes 2064384 | tf_op jit(solution)/shard_map/all_gather | solution.py:22
  7.9 140.0 %all-gather.10.cloned.1.call-start = ((), (), s32[]{:S(2)}) async-start(), calls=%async_computation.6 | async-start | bytes 2064384 | tf_op jit(solution)/shard_map/all_gather | solution.py:21
  8.7 207.0 %all-gather.6.cloned.1.call-start = ((), (), s32[]{:S(2)}) async-start(), calls=%async_computation.4 | async-start | bytes 2064384 | tf_op jit(solution)/shard_map/all_gather | solution.py:23
  9.4 292.1 %all-reduce.3.cloned.1.call-start = ((), (), s32[]{:S(2)}) async-start(), calls=%async_computation.10 | async-start | bytes 5505024 | tf_op jit(solution)/shard_map/psum | solution.py:28
  83.4 132.2 %copy-start.3 = (bf16[128,512]{1,0:T(8,128)(2,1)S(1)}, bf16[128,512]{1,0:T(8,128)(2,1)}, u32[]{:S(2)}) copy-start(bf16[128,512]{1,0:T(8,128)(2,1)} %param.6) | copy-start | bytes 393220
  303.7 10.8 %copy-start = (bf16[1792,512]{1,0:T(8,128)(2,1)S(1)}, bf16[1792,512]{1,0:T(8,128)(2,1)}, u32[]{:S(2)}) copy-start(bf16[1792,512]{1,0:T(8,128)(2,1)} %all-gather.10.cloned.1.call-done) | copy-start | bytes 5505028
  304.7 28.9 %all-to-all-start.1 = ((bf16[128,8,224]{0,2,1:T(8,128)(2,1)}), bf16[128,8,224]{0,2,1:T(8,128)(2,1)}, u32[]{:S(2)}, u32[]{:S(2)}) async-start(bf16[128,8,224]{0,2,1:T(8,128)(2,1)} %bitcast.2), calls=%async_computation.2 | async-start | bytes 917504 | tf_op jit(solution)/shard_map/all_to_all | solution.py:33
  314.4 123.1 %reduce-scatter.2.cloned.1.call-start = ((), (), s32[]{:S(2)}) async-start(), calls=%async_computation.7 | async-start | bytes 294912 | tf_op jit(solution)/shard_map/reduce_scatter | solution.py:36
  314.5 1.5 copy-start.1
  317.1 175.4 %all-gather.12.cloned.1.call-start = ((), (), s32[]{:S(2)}) async-start(), calls=%async_computation.8 | async-start | bytes 1179648 | tf_op jit(solution)/shard_map/all_gather | solution.py:17
  333.6 30.7 %all-to-all-start = ((bf16[128,8,224]{0,2,1:T(8,128)(2,1)}), bf16[128,8,224]{0,2,1:T(8,128)(2,1)S(1)}, u32[]{:S(2)}, u32[]{:S(2)}) async-start(bf16[128,8,224]{0,2,1:T(8,128)(2,1)} %bitcast), calls=%async_computation.1 | async-start | bytes 917504 | tf_op jit(solution)/shard_map/all_to_all | solution.py:32
  344.0 211.8 %all-gather.14.cloned.1.call-start = ((), (), s32[]{:S(2)}) async-start(), calls=%async_computation.9 | async-start | bytes 1179648 | tf_op jit(solution)/shard_map/all_gather | solution.py:18
  364.3 191.5 %all-to-all-start.2 = ((bf16[128,8,224]{0,2,1:T(8,128)(2,1)}), bf16[128,8,224]{0,2,1:T(8,128)(2,1)S(1)}, u32[]{:S(2)}, u32[]{:S(2)}) async-start(bf16[128,8,224]{0,2,1:T(8,128)(2,1)} %bitcast.4), calls=%async_computation.3 | async-start | bytes 917504 | tf_op jit(solution)/shard_map/all_to_all | solution.py:31
  492.5 2.5 copy-start.4
Sparse Core Ops, SparseCore 0:
  10.1 69.9 all-gather.7
  82.2 65.6 all-gather.9
  149.9 65.6 all-gather.5
  218.9 82.5 all-reduce.2
  320.0 117.4 reduce-scatter.1
  439.4 53.0 all-gather.11
  494.5 61.2 all-gather.13
where the time goes:
time: 571 us; the launch traced here: 565 us
  waiting for transfers between devices  495 us (87%)
  starting transfers between devices  31.2 us (5%)
  matrix products  17.1 us (3%)
  between operations  14.2 us (2%)
    psum x1, waiting for transfers between devices, body(): gate, up, hidden_grad = lax.psum((gate_part, up_part, grad_part), 'inp')  82.7 us
    all_gather x1, waiting for transfers between devices, body(): lax.all_gather(up_weight, 'dep', axis=0, tiled=True)  70.7 us
    all_gather x1, waiting for transfers between devices, body(): lax.all_gather(down_weight, 'dep', axis=0, tiled=True)  64.6 us
    all_gather x1, waiting for transfers between devices, body(): lax.all_gather(gate_weight, 'dep', axis=0, tiled=True)  64.4 us
    reduce_scatter x1, waiting for transfers between devices, body(): lax.psum_scatter(total + jnp.dot(up_delta, up_full, preferred_element_typ...  62.3 us
    all_gather x1, waiting for transfers between devices, body(): lax.all_gather(out_grad, 'dep', axis=0, tiled=True)  59.7 us
    all_gather x1, waiting for transfers between devices, body(): lax.all_gather(inputs, 'dep', axis=0, tiled=True)  53.6 us
    all_to_all x1, waiting for transfers between devices, body(): lax.all_to_all(gate_delta, 'dep', split_axis=1, concat_axis=0, tiled=True)  18.6 us
  transfers between devices with their start and end apart: 10, of which 9 were waited for; matrix products, arithmetic and copies ran while one was open for 3% of the time, Pallas kernels for 0%

commit v1 on v0

v1 whole, which is shorter than its diff:
```python
import functools

import jax
import jax.numpy as jnp
from jax import lax
from jax.experimental import pallas as pl
from jax.experimental.pallas import tpu as pltpu
from jax.sharding import PartitionSpec as P

MESH = pl.DeviceIdType.MESH
BF16, F32 = jnp.bfloat16, jnp.float32
T, R, H, HP, K = 128, 512, 224, 256, 16
CHUNKS = ((0,), (-1, 1), (-2, 2), (-3, 3), (4,))
N_SEM = 160


def kernel(
    x_hbm, g_hbm, wg_hbm, wu_hbm, wd_hbm, ig_out, gg_out, ug_out, dg_out,
    xg, gg, wgu, wd, acc, zr, zf, local_sem, send_sem, recv_sem, *bufs,
):
    inp, out, zl = lax.axis_index("inp"), lax.axis_index("out"), lax.axis_index("dep")
    x, c, y, zh = inp // 2, inp % 2, out % 4, out // 4
    z = zh * 8 + zl

    def at(dx=0, dc=0, dy=0, dz=0):
        zz = (z + dz) % 16
        return {
            "inp": ((x + dx) % 4) * 2 + (c + dc) % 2,
            "out": (zz // 8) * 4 + (y + dy) % 4,
            "dep": zz % 8,
        }

    partners = [dict(dc=1)] + [dict(dx=d) for d in (1, 2, 3)]
    partners += [dict(dy=d) for d in (1, 2, 3)] + [dict(dz=d) for d in range(1, 16)]

    pf, pb, cr, sf, xs, xr, hg, igf, igb, yr, zs = (
        bufs[i * len(CHUNKS) : (i + 1) * len(CHUNKS)] for i in range(11)
    )
    count = iter(range(N_SEM))
    sent = []

    def send(src, dst, where):
        i = next(count)
        copy = pltpu.make_async_remote_copy(
            src_ref=src, dst_ref=dst, send_sem=send_sem.at[i], recv_sem=recv_sem.at[i],
            device_id=at(**where), device_id_type=MESH,
        )
        copy.start()
        sent.append(copy)
        return copy

    local = []

    def fetch(src, dst):
        copy = pltpu.make_async_copy(src, dst, local_sem.at[len(local)])
        copy.start()
        local.append(copy)

    fetch(x_hbm, xg.at[zl])
    fetch(wg_hbm, wgu.at[pl.ds(0, H)])
    fetch(wu_hbm, wgu.at[pl.ds(HP, H)])
    fetch(wd_hbm, wd.at[pl.ds(0, H)])
    fetch(g_hbm, gg.at[zl])

    barrier = pltpu.get_barrier_semaphore()
    for where in partners:
        pl.semaphore_signal(barrier, inc=1, device_id=at(**where), device_id_type=MESH)
    wgu[H:HP, :] = jnp.zeros((HP - H, R), BF16)
    wgu[HP + H :, :] = jnp.zeros((HP - H, R), BF16)
    wd[H:, :] = jnp.zeros((HP - H, R), BF16)
    pl.semaphore_wait(barrier, len(partners))

    y32 = pl.multiple_of(y * 32, 32)

    def shard(d):
        return (zl + d + 8) % 8

    def span(piece, half):
        if piece < 2:
            return pl.ds(piece * 64, 64)
        if half is None:
            return pl.ds(y32, 32)
        return pl.ds(pl.multiple_of(y * 32 + half * 16, 16), 16)

    ring = {}

    def ring_send(k, piece):
        for way in (1, -1):
            half = None
            if k == 3:
                half = 0 if way == 1 else 1
                if piece < 2 and piece != half:
                    continue
            rows = span(piece, half)
            buf = gg if piece == 2 else xg
            dst = buf.at[shard(-way * k), rows]
            src = (g_hbm if piece == 2 else x_hbm).at[rows] if k == 0 else dst
            ring[k + 1, piece, way] = send(src, dst, dict(dz=way))

    ycopies, ccopies, xcopies, hcopies, dcopies, icopies, zcopies = ({} for _ in range(7))

    def start():
        for piece in (0, 2, 1):
            ring_send(0, piece)
        for copy in local:
            copy.wait()

    def arrive(k, piece):
        for way in (1, -1):
            if (k, piece, way) in ring:
                ring[k, piece, way].wait_recv()
        if k < 4:
            ring_send(k, piece)
        if piece == 2:
            for d in CHUNKS[k]:
                quarter = gg.at[shard(d), pl.ds(y32, 32)]
                for dy in (1, 2, 3):
                    ycopies[k, d, dy] = send(quarter, quarter, dict(dy=dy))

    def project(k, which):
        if which == 1 and k > 0:
            for d in CHUNKS[k]:
                for dy in (1, 2, 3):
                    ycopies[k, d, dy].wait_recv()
        w, buf = (wd, gg) if which else (wgu, xg)
        cols = slice(2 * HP, 3 * HP) if which else slice(0, 2 * HP)
        for i, d in enumerate(CHUNKS[k]):
            part = lax.dot_general(
                buf[shard(d)], w[...], (((1,), (1,)), ((), ())), preferred_element_type=F32
            ).reshape(2, 4, K, -1)
            pf[k][:, :, i, :, cols] = part
            pb[k][:, :, i, :, cols] = part.astype(BF16)
        if which:
            ccopies[k] = send(pb[k].at[1 - c], cr[k], dict(dc=1))

    def join_cores(k):
        ccopies[k].wait_recv()
        total = pf[k][c] + cr[k][...].astype(F32)
        sf[k][...] = total
        xs[k][...] = total.astype(BF16)
        for dx in (2, 1, 3):
            xcopies[k, dx] = send(xs[k].at[(x + dx) % 4], xr[k].at[dx - 1], dict(dx=dx))

    def activate(k):
        for dx in (1, 2, 3):
            xcopies[k, dx].wait_recv()
        total = sf[k][x]
        for dx in (1, 2, 3):
            total = total + xr[k][dx - 1].astype(F32)
        gate, up, grad = total[..., :HP], total[..., HP : 2 * HP], total[..., 2 * HP :]
        sig = jax.nn.sigmoid(gate)
        silu = gate * sig
        hg[k][c, x, :, :, 0:HP] = (silu * up).astype(BF16)
        hg[k][c, x, :, :, HP : 2 * HP] = (grad * up * sig * (1.0 + gate * (1.0 - sig))).astype(BF16)
        hg[k][c, x, :, :, 2 * HP :] = (grad * silu).astype(BF16)
        mine = hg[k].at[c, x]
        for dx in (2, 1, 3):
            hcopies[k, dx] = send(mine, mine, dict(dx=dx))

    def share(k):
        for dx in (1, 2, 3):
            hcopies[k, dx].wait_recv()
        dcopies[k] = send(hg[k].at[c], hg[k].at[c], dict(dc=1))

    def backward(k):
        dcopies[k].wait_recv()
        n = len(CHUNKS[k])
        delta = hg[k][..., HP:].reshape(n * T, 2 * HP)
        part = jnp.dot(delta, wgu[...], preferred_element_type=F32).reshape(2, 4, n, K, R)
        for h in range(2):
            igf[k][:, h] = part[h]
            igb[k][:, h] = part[h].astype(BF16)
        for dy in (2, 1, 3):
            icopies[k, dy] = send(igb[k].at[(y + dy) % 4], yr[k].at[dy - 1], dict(dy=dy))

    def weights(k):
        for i, d in enumerate(CHUNKS[k]):
            act = hg[k][:, :, i].reshape(T, 3 * HP)
            for cols, buf in ((slice(0, HP), gg), (slice(HP, 3 * HP), xg)):
                part = lax.dot_general(
                    act[:, cols], buf[shard(d)], (((0,), (0,)), ((), ())), preferred_element_type=F32
                )
                if k == 0:
                    acc[cols, :] = part
                else:
                    acc[cols, :] += part

    def spread(k):
        for dy in (1, 2, 3):
            icopies[k, dy].wait_recv()
        total = igf[k][y]
        for dy in (1, 2, 3):
            total = total + yr[k][dy - 1].astype(F32)
        zs[k][...] = total.astype(BF16)
        if k == 0:
            zf[...] = total[:, 0]
        for i, d in enumerate(CHUNKS[k]):
            for e in ((d + 8) % 16, d % 16):
                if e:
                    high = ((z + e) % 16) // 8
                    zcopies[e] = send(zs[k].at[high, i], zr.at[e - 1], dict(dz=e))

    def finish():
        total = zf[zh]
        for e in sorted(zcopies):
            zcopies[e].wait_recv()
        for e in sorted(zcopies):
            total = total + zr[e - 1].astype(F32)
        ig_out[...] = total.astype(BF16)

    def write():
        dg_out[...] = acc[0:H, :].astype(BF16)
        gg_out[...] = acc[HP : HP + H, :].astype(BF16)
        ug_out[...] = acc[2 * HP : 2 * HP + H, :].astype(BF16)

    start()
    project(0, 0)
    project(0, 1)
    last = len(CHUNKS) - 1
    for t in range(1, last + 7):
        if t <= last:
            arrive(t, 0)
            arrive(t, 2)
            arrive(t, 1)
        for stage, lag in ((spread, 6), (backward, 5), (share, 4), (activate, 3), (join_cores, 2)):
            k = t - lag
            if 0 <= k <= last:
                stage(k)
        if 0 <= t - 1 <= last and t > 1:
            project(t - 1, 0)
            project(t - 1, 1)
        k = t - 5
        if 0 <= k <= last:
            weights(k)
        if k == last:
            write()
    finish()
    for copy in sent:
        copy.wait_send()


def body(inputs, out_grad, gate_weight, up_weight, down_weight):
    any_spec = pl.BlockSpec(memory_space=pl.ANY)
    vmem_spec = pl.BlockSpec(memory_space=pltpu.VMEM)
    sizes = [len(c) for c in CHUNKS]

    def each(make):
        return [pltpu.VMEM(*make(n)) for n in sizes]

    wide = 3 * HP
    bufs = (
        each(lambda n: ((2, 4, n, K, wide), F32))
        + each(lambda n: ((2, 4, n, K, wide), BF16))
        + each(lambda n: ((4, n, K, wide), BF16))
        + each(lambda n: ((4, n, K, wide), F32))
        + each(lambda n: ((4, n, K, wide), BF16))
        + each(lambda n: ((3, n, K, wide), BF16))
        + each(lambda n: ((2, 4, n, K, wide), BF16))
        + each(lambda n: ((4, 2, n, K, R), F32))
        + each(lambda n: ((4, 2, n, K, R), BF16))
        + each(lambda n: ((3, 2, n, K, R), BF16))
        + each(lambda n: ((2, n, K, R), BF16))
    )
    return pl.pallas_call(
        kernel,
        out_shape=(
            jax.ShapeDtypeStruct((K, R), BF16),
            jax.ShapeDtypeStruct((H, R), BF16),
            jax.ShapeDtypeStruct((H, R), BF16),
            jax.ShapeDtypeStruct((H, R), BF16),
        ),
        in_specs=[any_spec] * 5,
        out_specs=(vmem_spec,) * 4,
        scratch_shapes=[
            pltpu.VMEM((8, T, R), BF16),
            pltpu.VMEM((8, T, R), BF16),
            pltpu.VMEM((2 * HP, R), BF16),
            pltpu.VMEM((HP, R), BF16),
            pltpu.VMEM((3 * HP, R), F32),
            pltpu.VMEM((15, K, R), BF16),
            pltpu.VMEM((2, K, R), F32),
            pltpu.SemaphoreType.DMA((5,)),
            pltpu.SemaphoreType.DMA((N_SEM,)),
            pltpu.SemaphoreType.DMA((N_SEM,)),
        ]
        + bufs,
        compiler_params=pltpu.CompilerParams(
            collective_id=0, has_side_effects=True, vmem_limit_bytes=56 * 2**20
        ),
        name="swiglu_backward",
    )(inputs, out_grad, gate_weight, up_weight, down_weight)


def solution(mesh):
    return jax.shard_map(
        body,
        mesh=mesh,
        in_specs=(
            P("dep", "inp"),
            P("dep", "inp"),
            P(("out", "dep"), "inp"),
            P(("out", "dep"), "inp"),
            P(("out", "dep"), "inp"),
        ),
        out_specs=(
            P(("dep", "out"), "inp"),
            P(("out", "dep"), "inp"),
            P(("out", "dep"), "inp"),
            P(("out", "dep"), "inp"),
        ),
        check_vma=False,
    )
```

time: 571 us -> 80.4 us (0.14)
  waiting for transfers between devices: 495 us -> 0 us
  Pallas kernels: 0 us -> 74.6 us
  starting transfers between devices: 31.2 us -> 0 us
  matrix products: 17.1 us -> 0 us
  between operations: 14.2 us -> 0.64 us
    all_gather x5 -> x0, waiting for transfers between devices: 313 us -> none  [the longest x1 70.7 us: body(): lax.all_gather(up_weight, 'dep', axis=0, tiled=True)]
    psum x1 -> x0, waiting for transfers between devices: 82.7 us -> none  [body(): gate, up, hidden_grad = lax.psum((gate_part, up_part, grad_part), 'inp')]
    pallas_call x0 -> x1, Pallas kernels: none -> 74.6 us  [body(): pl.pallas_call(kernel, out_shape=(jax.ShapeDtypeStruct((K, R), BF16), jax...]
    reduce_scatter x1 -> x0, waiting for transfers between devices: 62.3 us -> none  [body(): lax.psum_scatter(total + jnp.dot(up_delta, up_full, preferred_element_typ...]
    all_to_all x3 -> x0, waiting for transfers between devices: 33.6 us -> none  [the longest x1 18.6 us: body(): lax.all_to_all(gate_delta, 'dep', split_axis=1, concat_axis=0, tiled=True)]
    all_to_all x3 -> x0, starting transfers between devices: 30.9 us -> none  [the longest x1 10.9 us: body(): lax.all_to_all(hidden, 'dep', split_axis=1, concat_axis=0, tiled=True)]
    dot_general x8 -> x0, matrix products: 17.1 us -> none  [the longest x1 3.31 us: body(): jnp.einsum('tr,cr->tc', inputs, up_full, preferred_element_type=jnp.float32)]
  transfers between devices with their start and end apart: 10 -> 0, of which waited for: 9 -> 0; matrix products, arithmetic and copies ran while one was open for 3% -> 0% of each run, Pallas kernels for 0% -> 0%
where the time goes in v1:
time: 80.4 us; the launch traced here: 79.9 us
  Pallas kernels  74.6 us (93%)
  local copies, waits for them, and re-layouts  4.72 us (6%)
    pallas_call x1, Pallas kernels, body(): pl.pallas_call(kernel, out_shape=(jax.ShapeDtypeStruct((K, R), BF16), jax...  74.6 us
    unnamed x8, local copies, waits for them, and re-layouts  4.72 us

profile of v1, /device:TPU:1, one launch (start us, length us, event | category | flops | bytes accessed | tf_op | source)
XLA Modules:
  0.0 79.9 jit_solution(2124037103054277749)
XLA Ops:
  0.6 74.6 %swiglu_backward.1 = (bf16[16,512]{1,0:T(8,128)(2,1)}, bf16[224,512]{1,0:T(8,128)(2,1)}, bf16[224,512]{1,0:T(8,128)(2,1)}, bf16[224,512]{1,0:T(8,128)(2,1)}) custom-call(bf16[128,512]{1,0:T(8,128)(2,1)} %x_hbm.1, bf16[128,512]{1,0:T(8,128)(2,1)} %g_hbm.1, bf16[224,512]{1,0:T(8,128)(2,1)} %wg_hbm.1, bf16[224,512]{1,0:T(8,128)(2,1)} %wu_hbm.1, ...), custom_call_target="tpu_custom_call" | custom-call | tf_op jit(solution)/shard_map/swiglu_backward/pallas_call | solution.py:264
  75.2 1.3 %copy.13 = bf16[16,512]{1,0:T(8,128)(2,1)} copy(bf16[16,512]{1,0:T(8,128)(2,1)} %get-tuple-element.8) | data formatting | bytes 32768
  76.5 0.0 copy-start.1
  76.5 1.7 %copy.14 = bf16[224,512]{1,0:T(8,128)(2,1)} copy(bf16[224,512]{1,0:T(8,128)(2,1)} %get-tuple-element.9) | data formatting | bytes 458752
  78.2 0.0 copy-done.1
  78.2 0.0 copy-start
  78.2 0.7 copy.15
  78.9 0.3 copy-done
  79.2 0.7 copy.16
Async XLA Ops:
  76.5 1.7 %copy-start.1 = (bf16[224,512]{1,0:T(8,128)(2,1)S(1)}, bf16[224,512]{1,0:T(8,128)(2,1)}, u32[]{:S(2)}) copy-start(bf16[224,512]{1,0:T(8,128)(2,1)} %get-tuple-element.10) | copy-start | bytes 688132
  78.2 1.0 %copy-start = (bf16[224,512]{1,0:T(8,128)(2,1)S(1)}, bf16[224,512]{1,0:T(8,128)(2,1)}, u32[]{:S(2)}) copy-start(bf16[224,512]{1,0:T(8,128)(2,1)} %get-tuple-element.11) | copy-start | bytes 688132

commit v2 on v1

--- a/solution.py
+++ b/solution.py
@@ -10,13 +10,32 @@
 MESH = pl.DeviceIdType.MESH
 BF16, F32 = jnp.bfloat16, jnp.float32
 T, R, H, HP, K = 128, 512, 224, 256, 16
-CHUNKS = ((0,), (-1, 1), (-2, 2), (-3, 3), (4,))
+CHUNKS = ((0,), (-1,), (1,), (-2,), (2,), (-3,), (3,), (4,))
+PIECES = (2, 0, 1)
 N_SEM = 160
+
+
+ORDER = (
+    ("arrive", 1, 2), ("project_x", 0), ("project_g", 0), ("arrive", 1, 0), ("join_cores", 0),
+    ("arrive", 1, 1), ("project_x", 2), ("arrive", 2, 2), ("project_x", 1), ("project_g", 1),
+    ("arrive", 2, 0), ("join_cores", 1), ("activate", 0), ("project_g", 2), ("arrive", 2, 1),
+    ("project_x", 3), ("arrive", 3, 2), ("project_g", 3), ("join_cores", 2), ("project_x", 4),
+    ("join_cores", 3), ("project_g", 4), ("arrive", 3, 0), ("activate", 1), ("arrive", 3, 1),
+    ("join_cores", 4), ("share", 0), ("arrive", 4, 2), ("project_x", 5), ("project_g", 5), ("activate", 2),
+    ("project_x", 6), ("project_g", 6), ("activate", 3), ("arrive", 4, 1), ("arrive", 4, 0), ("backward", 0),
+    ("join_cores", 6), ("project_x", 7), ("join_cores", 5), ("project_g", 7), ("share", 1), ("activate", 4),
+    ("join_cores", 7), ("share", 3), ("backward", 1), ("activate", 6), ("share", 2), ("backward", 3),
+    ("spread", 0), ("activate", 5), ("backward", 2), ("share", 4), ("activate", 7), ("backward", 4),
+    ("weights", 4), ("share", 6), ("spread", 1), ("weights", 0), ("share", 5), ("backward", 6), ("spread", 3),
+    ("backward", 5), ("spread", 2), ("share", 7), ("spread", 4), ("backward", 7), ("weights", 1),
+    ("weights", 3), ("weights", 7), ("spread", 6), ("weights", 6), ("spread", 5), ("weights", 2),
+    ("weights", 5), ("spread", 7), ("write", 0), ("finish", 0),
+)
 
 
 def kernel(
     x_hbm, g_hbm, wg_hbm, wu_hbm, wd_hbm, ig_out, gg_out, ug_out, dg_out,
-    xg, gg, wgu, wd, acc, zr, zf, local_sem, send_sem, recv_sem, *bufs,
+    xg, gg, wgu, wd, acc, zr, zf, ig_buf, wbuf, local_sem, store_sem, send_sem, recv_sem, relay, *bufs,
 ):
     inp, out, zl = lax.axis_index("inp"), lax.axis_index("out"), lax.axis_index("dep")
     x, c, y, zh = inp // 2, inp % 2, out % 4, out // 4
@@ -31,10 +50,10 @@
         }
 
     partners = [dict(dc=1)] + [dict(dx=d) for d in (1, 2, 3)]
-    partners += [dict(dy=d) for d in (1, 2, 3)] + [dict(dz=d) for d in range(1, 16)]
-
-    pf, pb, cr, sf, xs, xr, hg, igf, igb, yr, zs = (
-        bufs[i * len(CHUNKS) : (i + 1) * len(CHUNKS)] for i in range(11)
+    partners += [dict(dy=d) for d in (1, 2, 3)] + [dict(dz=d) for d in (1, 15)]
+
+    pf, cr, sf, xs, xr, hg, igf, igb, yr, zs = (
+        bufs[i * len(CHUNKS) : (i + 1) * len(CHUNKS)] for i in range(10)
     )
     count = iter(range(N_SEM))
     sent = []
@@ -48,6 +67,13 @@
         copy.start()
         sent.append(copy)
         return copy
+
+    stored = []
+
+    def store(src, dst):
+        copy = pltpu.make_async_copy(src, dst, store_sem.at[len(stored)])
+        copy.start()
+        stored.append(copy)
 
     local = []
 
@@ -97,10 +123,11 @@
             src = (g_hbm if piece == 2 else x_hbm).at[rows] if k == 0 else dst
             ring[k + 1, piece, way] = send(src, dst, dict(dz=way))
 
+    weighed, spreads = [], []
     ycopies, ccopies, xcopies, hcopies, dcopies, icopies, zcopies = ({} for _ in range(7))
 
     def start():
-        for piece in (0, 2, 1):
+        for piece in PIECES:
             ring_send(0, piece)
         for copy in local:
             copy.wait()
@@ -111,17 +138,20 @@
                 ring[k, piece, way].wait_recv()
         if k < 4:
             ring_send(k, piece)
+        elif piece == 2:
+            for way in (4, 12):
+                pl.semaphore_signal(relay, inc=1, device_id=at(dz=way), device_id_type=MESH)
         if piece == 2:
-            for d in CHUNKS[k]:
+            for d in (-k, k) if k < 4 else (4,):
                 quarter = gg.at[shard(d), pl.ds(y32, 32)]
                 for dy in (1, 2, 3):
-                    ycopies[k, d, dy] = send(quarter, quarter, dict(dy=dy))
+                    ycopies[d, dy] = send(quarter, quarter, dict(dy=dy))
 
     def project(k, which):
         if which == 1 and k > 0:
             for d in CHUNKS[k]:
                 for dy in (1, 2, 3):
-                    ycopies[k, d, dy].wait_recv()
+                    ycopies[d, dy].wait_recv()
         w, buf = (wd, gg) if which else (wgu, xg)
         cols = slice(2 * HP, 3 * HP) if which else slice(0, 2 * HP)
         for i, d in enumerate(CHUNKS[k]):
@@ -129,13 +159,12 @@
                 buf[shard(d)], w[...], (((1,), (1,)), ((), ())), preferred_element_type=F32
             ).reshape(2, 4, K, -1)
             pf[k][:, :, i, :, cols] = part
-            pb[k][:, :, i, :, cols] = part.astype(BF16)
         if which:
-            ccopies[k] = send(pb[k].at[1 - c], cr[k], dict(dc=1))
+            ccopies[k] = send(pf[k].at[1 - c], cr[k], dict(dc=1))
 
     def join_cores(k):
         ccopies[k].wait_recv()
-        total = pf[k][c] + cr[k][...].astype(F32)
+        total = pf[k][c] + cr[k][...]
         sf[k][...] = total
         xs[k][...] = total.astype(BF16)
         for dx in (2, 1, 3):
@@ -180,10 +209,11 @@
                 part = lax.dot_general(
                     act[:, cols], buf[shard(d)], (((0,), (0,)), ((), ())), preferred_element_type=F32
                 )
-                if k == 0:
+                if not weighed:
                     acc[cols, :] = part
                 else:
                     acc[cols, :] += part
+        weighed.append(k)
 
     def spread(k):
         for dy in (1, 2, 3):
@@ -192,6 +222,9 @@
         for dy in (1, 2, 3):
             total = total + yr[k][dy - 1].astype(F32)
         zs[k][...] = total.astype(BF16)
+        if not spreads:
+            pl.semaphore_wait(relay, 2)
+        spreads.append(k)
         if k == 0:
             zf[...] = total[:, 0]
         for i, d in enumerate(CHUNKS[k]):
@@ -206,42 +239,43 @@
             zcopies[e].wait_recv()
         for e in sorted(zcopies):
             total = total + zr[e - 1].astype(F32)
-        ig_out[...] = total.astype(BF16)
+        ig_buf[...] = total.astype(BF16)
+        store(ig_buf, ig_out)
 
     def write():
-        dg_out[...] = acc[0:H, :].astype(BF16)
-        gg_out[...] = acc[HP : HP + H, :].astype(BF16)
-        ug_out[...] = acc[2 * HP : 2 * HP + H, :].astype(BF16)
+        for i, result in enumerate((dg_out, gg_out, ug_out)):
+            wbuf[i] = acc[i * HP : i * HP + H, :].astype(BF16)
+            store(wbuf.at[i], result)
 
     start()
-    project(0, 0)
-    project(0, 1)
-    last = len(CHUNKS) - 1
-    for t in range(1, last + 7):
-        if t <= last:
-            arrive(t, 0)
-            arrive(t, 2)
-            arrive(t, 1)
-        for stage, lag in ((spread, 6), (backward, 5), (share, 4), (activate, 3), (join_cores, 2)):
-            k = t - lag
-            if 0 <= k <= last:
-                stage(k)
-        if 0 <= t - 1 <= last and t > 1:
-            project(t - 1, 0)
-            project(t - 1, 1)
-        k = t - 5
-        if 0 <= k <= last:
-            weights(k)
-        if k == last:
-            write()
-    finish()
+    steps = dict(
+        arrive=arrive, project_x=lambda k: project(k, 0), project_g=lambda k: project(k, 1),
+        join_cores=join_cores, activate=activate, share=share, backward=backward,
+        weights=weights, spread=spread, write=lambda k: write(), finish=lambda k: finish(),
+    )
+    for name, *where in ORDER:
+        steps[name](*where)
     for copy in sent:
         copy.wait_send()
+    for copy in stored:
+        copy.wait()
+
+
+def land(*refs):
+    sources, results, held, sem_in, sem_out = refs[:4], refs[4:8], refs[8:12], refs[12], refs[13]
+    loads = [pltpu.make_async_copy(sources[i], held[i], sem_in.at[i]) for i in range(4)]
+    stores = [pltpu.make_async_copy(held[i], results[i], sem_out.at[i]) for i in range(4)]
+    for load in loads:
+        load.start()
+    for load, store in zip(loads, stores):
+        load.wait()
+        store.start()
+    for store in stores:
+        store.wait()
 
 
 def body(inputs, out_grad, gate_weight, up_weight, down_weight):
     any_spec = pl.BlockSpec(memory_space=pl.ANY)
-    vmem_spec = pl.BlockSpec(memory_space=pltpu.VMEM)
     sizes = [len(c) for c in CHUNKS]
 
     def each(make):
@@ -250,8 +284,7 @@
     wide = 3 * HP
     bufs = (
         each(lambda n: ((2, 4, n, K, wide), F32))
-        + each(lambda n: ((2, 4, n, K, wide), BF16))
-        + each(lambda n: ((4, n, K, wide), BF16))
+        + each(lambda n: ((4, n, K, wide), F32))
         + each(lambda n: ((4, n, K, wide), F32))
         + each(lambda n: ((4, n, K, wide), BF16))
         + each(lambda n: ((3, n, K, wide), BF16))
@@ -261,7 +294,7 @@
         + each(lambda n: ((3, 2, n, K, R), BF16))
         + each(lambda n: ((2, n, K, R), BF16))
     )
-    return pl.pallas_call(
+    parts = pl.pallas_call(
         kernel,
         out_shape=(
             jax.ShapeDtypeStruct((K, R), BF16),
@@ -270,7 +303,7 @@
             jax.ShapeDtypeStruct((H, R), BF16),
         ),
         in_specs=[any_spec] * 5,
-        out_specs=(vmem_spec,) * 4,
+        out_specs=(any_spec,) * 4,
         scratch_shapes=[
             pltpu.VMEM((8, T, R), BF16),
             pltpu.VMEM((8, T, R), BF16),
@@ -279,9 +312,13 @@
             pltpu.VMEM((3 * HP, R), F32),
             pltpu.VMEM((15, K, R), BF16),
             pltpu.VMEM((2, K, R), F32),
+            pltpu.VMEM((K, R), BF16),
+            pltpu.VMEM((3, H, R), BF16),
             pltpu.SemaphoreType.DMA((5,)),
+            pltpu.SemaphoreType.DMA((4,)),
             pltpu.SemaphoreType.DMA((N_SEM,)),
             pltpu.SemaphoreType.DMA((N_SEM,)),
+            pltpu.SemaphoreType.REGULAR,
         ]
         + bufs,
         compiler_params=pltpu.CompilerParams(
@@ -289,6 +326,17 @@
         ),
         name="swiglu_backward",
     )(inputs, out_grad, gate_weight, up_weight, down_weight)
+    return tuple(
+        pl.pallas_call(
+            land,
+            out_shape=tuple(jax.ShapeDtypeStruct(p.shape, p.dtype) for p in parts),
+            in_specs=[any_spec] * 4,
+            out_specs=(any_spec,) * 4,
+            scratch_shapes=[pltpu.VMEM(p.shape, p.dtype) for p in parts]
+            + [pltpu.SemaphoreType.DMA((4,)), pltpu.SemaphoreType.DMA((4,))],
+            name="land",
+        )(*parts)
+    )
 
 
 def solution(mesh):

time: 80.4 us -> 62.6 us (0.78)
  Pallas kernels: 74.6 us -> 61.7 us
  local copies, waits for them, and re-layouts: 4.72 us -> 0 us
    pallas_call x1, Pallas kernels: 74.6 us -> 59.8 us  [body(): pl.pallas_call(kernel, out_shape=(jax.ShapeDtypeStruct((K, R), BF16), jax...]
    unnamed x8 -> x0, local copies, waits for them, and re-layouts: 4.72 us -> none
    pallas_call x0 -> x1, Pallas kernels: none -> 1.93 us  [body(): pl.pallas_call(land, out_shape=tuple((jax.ShapeDtypeStruct(p.shape, p.dty...]
where the time goes in v2:
time: 62.6 us; the launch traced here: 62.4 us
  Pallas kernels  61.7 us (99%)
  between operations  0.64 us (1%)
    pallas_call x1, Pallas kernels, body(): pl.pallas_call(kernel, out_shape=(jax.ShapeDtypeStruct((K, R), BF16), jax...  59.8 us
    pallas_call x1, Pallas kernels, body(): pl.pallas_call(land, out_shape=tuple((jax.ShapeDtypeStruct(p.shape, p.dty...  1.93 us

profile of v2, /device:TPU:1, one launch (start us, length us, event | category | flops | bytes accessed | tf_op | source)
XLA Modules:
  0.0 62.4 jit_solution(15387994551920654762)
XLA Ops:
  0.6 59.8 %swiglu_backward.1 = (bf16[16,512]{1,0:T(8,128)(2,1)}, bf16[224,512]{1,0:T(8,128)(2,1)}, bf16[224,512]{1,0:T(8,128)(2,1)}, bf16[224,512]{1,0:T(8,128)(2,1)}) custom-call(bf16[128,512]{1,0:T(8,128)(2,1)} %x_hbm.1, bf16[128,512]{1,0:T(8,128)(2,1)} %g_hbm.1, bf16[224,512]{1,0:T(8,128)(2,1)} %wg_hbm.1, bf16[224,512]{1,0:T(8,128)(2,1)} %wu_hbm.1, ...), custom_call_target="tpu_custom_call" | custom-call | tf_op jit(solution)/shard_map/swiglu_backward/pallas_call | solution.py:297
  60.4 1.9 %land.1 = (bf16[16,512]{1,0:T(8,128)(2,1)}, bf16[224,512]{1,0:T(8,128)(2,1)}, bf16[224,512]{1,0:T(8,128)(2,1)}, bf16[224,512]{1,0:T(8,128)(2,1)}) custom-call(bf16[16,512]{1,0:T(8,128)(2,1)} %get-tuple-element.8.refs_0_, bf16[224,512]{1,0:T(8,128)(2,1)} %get-tuple-element.9.refs_1_, bf16[224,512]{1,0:T(8,128)(2,1)} %get-tuple-element.10.refs_2_, ...), custom_call_target="tpu_custom_call" | custom-call | tf_op jit(solution)/shard_map/land/pallas_call | solution.py:330

commit v3 on v2

--- a/solution.py
+++ b/solution.py
@@ -16,20 +16,22 @@
 
 
 ORDER = (
-    ("arrive", 1, 2), ("project_x", 0), ("project_g", 0), ("arrive", 1, 0), ("join_cores", 0),
-    ("arrive", 1, 1), ("project_x", 2), ("arrive", 2, 2), ("project_x", 1), ("project_g", 1),
-    ("arrive", 2, 0), ("join_cores", 1), ("activate", 0), ("project_g", 2), ("arrive", 2, 1),
-    ("project_x", 3), ("arrive", 3, 2), ("project_g", 3), ("join_cores", 2), ("project_x", 4),
-    ("join_cores", 3), ("project_g", 4), ("arrive", 3, 0), ("activate", 1), ("arrive", 3, 1),
-    ("join_cores", 4), ("share", 0), ("arrive", 4, 2), ("project_x", 5), ("project_g", 5), ("activate", 2),
-    ("project_x", 6), ("project_g", 6), ("activate", 3), ("arrive", 4, 1), ("arrive", 4, 0), ("backward", 0),
-    ("join_cores", 6), ("project_x", 7), ("join_cores", 5), ("project_g", 7), ("share", 1), ("activate", 4),
-    ("join_cores", 7), ("share", 3), ("backward", 1), ("activate", 6), ("share", 2), ("backward", 3),
-    ("spread", 0), ("activate", 5), ("backward", 2), ("share", 4), ("activate", 7), ("backward", 4),
-    ("weights", 4), ("share", 6), ("spread", 1), ("weights", 0), ("share", 5), ("backward", 6), ("spread", 3),
-    ("backward", 5), ("spread", 2), ("share", 7), ("spread", 4), ("backward", 7), ("weights", 1),
-    ("weights", 3), ("weights", 7), ("spread", 6), ("weights", 6), ("spread", 5), ("weights", 2),
-    ("weights", 5), ("spread", 7), ("write", 0), ("finish", 0),
+    ("project_x", 0), ("arrive", 1, 2, 1), ("arrive", 1, 2, -1), ("project_g", 0), ("arrive", 1, 0, 1),
+    ("arrive", 1, 0, -1), ("join_cores", 0), ("arrive", 1, 1, 1), ("arrive", 1, 1, -1), ("project_x", 1),
+    ("arrive", 2, 2, 1), ("arrive", 2, 2, -1), ("project_x", 2), ("project_g", 1), ("arrive", 2, 0, 1),
+    ("arrive", 2, 0, -1), ("project_g", 2), ("join_cores", 1), ("activate", 0), ("arrive", 2, 1, 1),
+    ("arrive", 2, 1, -1), ("project_x", 3), ("join_cores", 2), ("project_g", 3), ("arrive", 3, 2, 1),
+    ("arrive", 3, 2, -1), ("project_x", 4), ("join_cores", 3), ("project_g", 4), ("arrive", 3, 0, 1),
+    ("arrive", 3, 0, -1), ("activate", 1), ("arrive", 3, 1, 1), ("arrive", 3, 1, -1), ("project_x", 5),
+    ("join_cores", 4), ("arrive", 4, 2, 1), ("arrive", 4, 2, -1), ("activate", 2), ("project_x", 6),
+    ("project_g", 5), ("activate", 3), ("share", 0), ("project_g", 6), ("join_cores", 5), ("arrive", 4, 0, 1),
+    ("arrive", 4, 1, -1), ("project_x", 7), ("join_cores", 6), ("project_g", 7), ("share", 1),
+    ("backward", 0), ("share", 2), ("activate", 4), ("join_cores", 7), ("backward", 1), ("share", 3),
+    ("backward", 2), ("activate", 5), ("backward", 3), ("activate", 6), ("share", 4), ("spread", 0),
+    ("activate", 7), ("backward", 4), ("share", 5), ("spread", 1), ("weights", 1), ("spread", 2),
+    ("share", 6), ("backward", 5), ("spread", 3), ("backward", 6), ("share", 7), ("weights", 5),
+    ("spread", 4), ("backward", 7), ("weights", 0), ("spread", 5), ("weights", 7), ("weights", 3),
+    ("spread", 6), ("weights", 6), ("spread", 7), ("finish", 0), ("weights", 2), ("weights", 4), ("write", 0),
 )
 
 
@@ -49,8 +51,8 @@
             "dep": zz % 8,
         }
 
-    partners = [dict(dc=1)] + [dict(dx=d) for d in (1, 2, 3)]
-    partners += [dict(dy=d) for d in (1, 2, 3)] + [dict(dz=d) for d in (1, 15)]
+    partners = [dict(dz=1), dict(dz=15), dict(dc=1)]
+    partners += [dict(dx=d) for d in (1, 2, 3)] + [dict(dy=d) for d in (1, 2, 3)]
 
     pf, cr, sf, xs, xr, hg, igf, igb, yr, zs = (
         bufs[i * len(CHUNKS) : (i + 1) * len(CHUNKS)] for i in range(10)
@@ -82,15 +84,14 @@
         copy.start()
         local.append(copy)
 
+    barrier = pltpu.get_barrier_semaphore()
+    for where in partners:
+        pl.semaphore_signal(barrier, inc=1, device_id=at(**where), device_id_type=MESH)
     fetch(x_hbm, xg.at[zl])
     fetch(wg_hbm, wgu.at[pl.ds(0, H)])
     fetch(wu_hbm, wgu.at[pl.ds(HP, H)])
     fetch(wd_hbm, wd.at[pl.ds(0, H)])
     fetch(g_hbm, gg.at[zl])
-
-    barrier = pltpu.get_barrier_semaphore()
-    for where in partners:
-        pl.semaphore_signal(barrier, inc=1, device_id=at(**where), device_id_type=MESH)
     wgu[H:HP, :] = jnp.zeros((HP - H, R), BF16)
     wgu[HP + H :, :] = jnp.zeros((HP - H, R), BF16)
     wd[H:, :] = jnp.zeros((HP - H, R), BF16)
@@ -110,42 +111,40 @@
 
     ring = {}
 
-    def ring_send(k, piece):
-        for way in (1, -1):
-            half = None
-            if k == 3:
-                half = 0 if way == 1 else 1
-                if piece < 2 and piece != half:
-                    continue
-            rows = span(piece, half)
-            buf = gg if piece == 2 else xg
-            dst = buf.at[shard(-way * k), rows]
-            src = (g_hbm if piece == 2 else x_hbm).at[rows] if k == 0 else dst
-            ring[k + 1, piece, way] = send(src, dst, dict(dz=way))
+    def ring_send(k, piece, way):
+        half = None
+        if k == 3:
+            half = 0 if way == 1 else 1
+            if piece < 2 and piece != half:
+                return
+        rows = span(piece, half)
+        buf = gg if piece == 2 else xg
+        dst = buf.at[shard(-way * k), rows]
+        src = (g_hbm if piece == 2 else x_hbm).at[rows] if k == 0 else dst
+        ring[k + 1, piece, way] = send(src, dst, dict(dz=way))
 
     weighed, spreads = [], []
     ycopies, ccopies, xcopies, hcopies, dcopies, icopies, zcopies = ({} for _ in range(7))
 
     def start():
         for piece in PIECES:
-            ring_send(0, piece)
+            for way in (1, -1):
+                ring_send(0, piece, way)
         for copy in local:
             copy.wait()
 
-    def arrive(k, piece):
-        for way in (1, -1):
-            if (k, piece, way) in ring:
-                ring[k, piece, way].wait_recv()
+    def arrive(k, piece, way):
+        ring[k, piece, way].wait_recv()
         if k < 4:
-            ring_send(k, piece)
-        elif piece == 2:
-            for way in (4, 12):
-                pl.semaphore_signal(relay, inc=1, device_id=at(dz=way), device_id_type=MESH)
-        if piece == 2:
-            for d in (-k, k) if k < 4 else (4,):
-                quarter = gg.at[shard(d), pl.ds(y32, 32)]
-                for dy in (1, 2, 3):
-                    ycopies[d, dy] = send(quarter, quarter, dict(dy=dy))
+            ring_send(k, piece, way)
+        if piece == 2 and (k < 4 or way == -1):
+            d = -way * k if k < 4 else 4
+            quarter = gg.at[shard(d), pl.ds(y32, 32)]
+            for dy in (2, 1, 3):
+                ycopies[d, dy] = send(quarter, quarter, dict(dy=dy))
+        if k == 4 and piece == 2 and way == -1:
+            for far in (4, 12):
+                pl.semaphore_signal(relay, inc=1, device_id=at(dz=far), device_id_type=MESH)
 
     def project(k, which):
         if which == 1 and k > 0:
@@ -234,6 +233,9 @@
                     zcopies[e] = send(zs[k].at[high, i], zr.at[e - 1], dict(dz=e))
 
     def finish():
+        for copy in sent:
+            if all(copy is not q for q in zcopies.values()):
+                copy.wait_send()
         total = zf[zh]
         for e in sorted(zcopies):
             zcopies[e].wait_recv()
@@ -255,7 +257,7 @@
     )
     for name, *where in ORDER:
         steps[name](*where)
-    for copy in sent:
+    for copy in zcopies.values():
         copy.wait_send()
     for copy in stored:
         copy.wait()

time: 62.6 us -> 60.6 us (0.968)
  Pallas kernels: 61.7 us -> 59.8 us
    pallas_call x1, Pallas kernels: 59.8 us -> 57.9 us  [body(): pl.pallas_call(kernel, out_shape=(jax.ShapeDtypeStruct((K, R), BF16), jax...]
where the time goes in v3:
time: 60.6 us; the launch traced here: 60.4 us
  Pallas kernels  59.8 us (99%)
  between operations  0.64 us (1%)
    pallas_call x1, Pallas kernels, body(): pl.pallas_call(kernel, out_shape=(jax.ShapeDtypeStruct((K, R), BF16), jax...  57.9 us
    pallas_call x1, Pallas kernels, body(): pl.pallas_call(land, out_shape=tuple((jax.ShapeDtypeStruct(p.shape, p.dty...  1.93 us

profile of v3, /device:TPU:1, one launch (start us, length us, event | category | flops | bytes accessed | tf_op | source)
XLA Modules:
  0.0 60.4 jit_solution(10289407634512965576)
XLA Ops:
  0.6 57.9 %swiglu_backward.1 = (bf16[16,512]{1,0:T(8,128)(2,1)}, bf16[224,512]{1,0:T(8,128)(2,1)}, bf16[224,512]{1,0:T(8,128)(2,1)}, bf16[224,512]{1,0:T(8,128)(2,1)}) custom-call(bf16[128,512]{1,0:T(8,128)(2,1)} %x_hbm.1, bf16[128,512]{1,0:T(8,128)(2,1)} %g_hbm.1, bf16[224,512]{1,0:T(8,128)(2,1)} %wg_hbm.1, bf16[224,512]{1,0:T(8,128)(2,1)} %wu_hbm.1, ...), custom_call_target="tpu_custom_call" | custom-call | tf_op jit(solution)/shard_map/swiglu_backward/pallas_call | solution.py:299
  58.5 1.9 %land.1 = (bf16[16,512]{1,0:T(8,128)(2,1)}, bf16[224,512]{1,0:T(8,128)(2,1)}, bf16[224,512]{1,0:T(8,128)(2,1)}, bf16[224,512]{1,0:T(8,128)(2,1)}) custom-call(bf16[16,512]{1,0:T(8,128)(2,1)} %get-tuple-element.8.refs_0_, bf16[224,512]{1,0:T(8,128)(2,1)} %get-tuple-element.9.refs_1_, bf16[224,512]{1,0:T(8,128)(2,1)} %get-tuple-element.10.refs_2_, ...), custom_call_target="tpu_custom_call" | custom-call | tf_op jit(solution)/shard_map/land/pallas_call | solution.py:332

commit v4 on v3

--- a/solution.py
+++ b/solution.py
@@ -16,28 +16,28 @@
 
 
 ORDER = (
-    ("project_x", 0), ("arrive", 1, 2, 1), ("arrive", 1, 2, -1), ("project_g", 0), ("arrive", 1, 0, 1),
-    ("arrive", 1, 0, -1), ("join_cores", 0), ("arrive", 1, 1, 1), ("arrive", 1, 1, -1), ("project_x", 1),
-    ("arrive", 2, 2, 1), ("arrive", 2, 2, -1), ("project_x", 2), ("project_g", 1), ("arrive", 2, 0, 1),
-    ("arrive", 2, 0, -1), ("project_g", 2), ("join_cores", 1), ("activate", 0), ("arrive", 2, 1, 1),
-    ("arrive", 2, 1, -1), ("project_x", 3), ("join_cores", 2), ("project_g", 3), ("arrive", 3, 2, 1),
-    ("arrive", 3, 2, -1), ("project_x", 4), ("join_cores", 3), ("project_g", 4), ("arrive", 3, 0, 1),
-    ("arrive", 3, 0, -1), ("activate", 1), ("arrive", 3, 1, 1), ("arrive", 3, 1, -1), ("project_x", 5),
-    ("join_cores", 4), ("arrive", 4, 2, 1), ("arrive", 4, 2, -1), ("activate", 2), ("project_x", 6),
-    ("project_g", 5), ("activate", 3), ("share", 0), ("project_g", 6), ("join_cores", 5), ("arrive", 4, 0, 1),
-    ("arrive", 4, 1, -1), ("project_x", 7), ("join_cores", 6), ("project_g", 7), ("share", 1),
-    ("backward", 0), ("share", 2), ("activate", 4), ("join_cores", 7), ("backward", 1), ("share", 3),
-    ("backward", 2), ("activate", 5), ("backward", 3), ("activate", 6), ("share", 4), ("spread", 0),
-    ("activate", 7), ("backward", 4), ("share", 5), ("spread", 1), ("weights", 1), ("spread", 2),
-    ("share", 6), ("backward", 5), ("spread", 3), ("backward", 6), ("share", 7), ("weights", 5),
-    ("spread", 4), ("backward", 7), ("weights", 0), ("spread", 5), ("weights", 7), ("weights", 3),
-    ("spread", 6), ("weights", 6), ("spread", 7), ("finish", 0), ("weights", 2), ("weights", 4), ("write", 0),
+    ("project_x", 0), ("arrive", 1, 2, 1), ("arrive", 1, 2, -1), ("arrive", 1, 0, 1), ("arrive", 1, 0, -1),
+    ("project_g", 0), ("arrive", 1, 1, -1), ("arrive", 1, 1, 1), ("arrive", 2, 2, 1), ("project_x", 1),
+    ("join_cores", 0), ("project_g", 1), ("project_x", 2), ("arrive", 2, 2, -1), ("arrive", 2, 0, 1),
+    ("arrive", 2, 0, -1), ("project_g", 2), ("join_cores", 1), ("arrive", 2, 1, 1), ("arrive", 2, 1, -1),
+    ("project_x", 3), ("join_cores", 2), ("arrive", 3, 2, 1), ("project_g", 3), ("arrive", 3, 2, -1),
+    ("activate", 0), ("project_x", 4), ("arrive", 3, 0, 1), ("join_cores", 3), ("activate", 1),
+    ("arrive", 3, 0, -1), ("project_g", 4), ("arrive", 3, 1, -1), ("arrive", 4, 2, 1), ("arrive", 4, 2, -1),
+    ("activate", 2), ("arrive", 3, 1, 1), ("project_x", 5), ("project_g", 5), ("join_cores", 4),
+    ("project_x", 6), ("activate", 3), ("project_g", 6), ("arrive", 4, 0, 1), ("join_cores", 5), ("share", 1),
+    ("share", 0), ("arrive", 4, 1, -1), ("project_x", 7), ("project_g", 7), ("join_cores", 6),
+    ("backward", 1), ("share", 2), ("backward", 0), ("join_cores", 7), ("activate", 4), ("backward", 2),
+    ("activate", 5), ("weights", 1), ("share", 3), ("backward", 3), ("activate", 6), ("spread", 1),
+    ("activate", 7), ("weights", 0), ("share", 4), ("backward", 4), ("spread", 0), ("spread", 2),
+    ("share", 5), ("backward", 5), ("spread", 3), ("share", 6), ("backward", 6), ("weights", 3), ("share", 7),
+    ("weights", 4), ("backward", 7), ("spread", 4), ("weights", 5), ("spread", 5), ("weights", 7),
+    ("weights", 6), ("spread", 6), ("spread", 7), ("finish", 0), ("weights", 2), ("write", 0),
 )
 
 
 def kernel(
     x_hbm, g_hbm, wg_hbm, wu_hbm, wd_hbm, ig_out, gg_out, ug_out, dg_out,
-    xg, gg, wgu, wd, acc, zr, zf, ig_buf, wbuf, local_sem, store_sem, send_sem, recv_sem, relay, *bufs,
+    xg, gg, wgu, wd, wother, acc, zr, zsend_sem, zrecv_sem, ig_buf, wbuf, local_sem, store_sem, send_sem, recv_sem, relay, *bufs,
 ):
     inp, out, zl = lax.axis_index("inp"), lax.axis_index("out"), lax.axis_index("dep")
     x, c, y, zh = inp // 2, inp % 2, out % 4, out // 4
@@ -123,7 +123,7 @@
         src = (g_hbm if piece == 2 else x_hbm).at[rows] if k == 0 else dst
         ring[k + 1, piece, way] = send(src, dst, dict(dz=way))
 
-    weighed, spreads = [], []
+    weighed, spreads, other = [], [], []
     ycopies, ccopies, xcopies, hcopies, dcopies, icopies, zcopies = ({} for _ in range(7))
 
     def start():
@@ -132,6 +132,7 @@
                 ring_send(0, piece, way)
         for copy in local:
             copy.wait()
+        other.append(send(wgu, wother, dict(dc=1)))
 
     def arrive(k, piece, way):
         ring[k, piece, way].wait_recv()
@@ -191,17 +192,20 @@
         dcopies[k] = send(hg[k].at[c], hg[k].at[c], dict(dc=1))
 
     def backward(k):
-        dcopies[k].wait_recv()
+        if len(other) == 1:
+            other[0].wait_recv()
+            other.append(k)
         n = len(CHUNKS[k])
-        delta = hg[k][..., HP:].reshape(n * T, 2 * HP)
-        part = jnp.dot(delta, wgu[...], preferred_element_type=F32).reshape(2, 4, n, K, R)
-        for h in range(2):
-            igf[k][:, h] = part[h]
-            igb[k][:, h] = part[h].astype(BF16)
+        delta = hg[k][c, :, :, :, HP:].reshape(n * T // 2, 2 * HP)
+        for f, w in enumerate((wgu, wother)):
+            part = jnp.dot(delta, w[...], preferred_element_type=F32).reshape(4, n, K, R)
+            igf[k][:, f] = part
+            igb[k][:, f] = part.astype(BF16)
         for dy in (2, 1, 3):
             icopies[k, dy] = send(igb[k].at[(y + dy) % 4], yr[k].at[dy - 1], dict(dy=dy))
 
     def weights(k):
+        dcopies[k].wait_recv()
         for i, d in enumerate(CHUNKS[k]):
             act = hg[k][:, :, i].reshape(T, 3 * HP)
             for cols, buf in ((slice(0, HP), gg), (slice(HP, 3 * HP), xg)):
@@ -224,23 +228,50 @@
         if not spreads:
             pl.semaphore_wait(relay, 2)
         spreads.append(k)
-        if k == 0:
-            zf[...] = total[:, 0]
         for i, d in enumerate(CHUNKS[k]):
-            for e in ((d + 8) % 16, d % 16):
-                if e:
-                    high = ((z + e) % 16) // 8
-                    zcopies[e] = send(zs[k].at[high, i], zr.at[e - 1], dict(dz=e))
+            for f in range(2):
+                zsend(k, f, zs[k].at[f, i], d)
+
+    def zcopy(k, f, src, d):
+        slot = 2 * k + zh
+        return pltpu.make_async_remote_copy(
+            src_ref=src, dst_ref=zr.at[slot], send_sem=zsend_sem.at[2 * k + f], recv_sem=zrecv_sem.at[slot],
+            device_id={"inp": x * 2 + (c + f) % 2, "out": c * 4 + y, "dep": (zl + d + 8) % 8},
+            device_id_type=MESH,
+        )
+
+    def zsend(k, f, src, d):
+        copy = zcopy(k, f, src, d)
+        zcopies[k, f] = copy
+        if k or f:
+            copy.start()
+            return
+
+        @pl.when(zh != c)
+        def _():
+            copy.start()
+
+        @pl.when(zh == c)
+        def _():
+            zr[zh] = src[...]
 
     def finish():
         for copy in sent:
-            if all(copy is not q for q in zcopies.values()):
-                copy.wait_send()
-        total = zf[zh]
-        for e in sorted(zcopies):
-            zcopies[e].wait_recv()
-        for e in sorted(zcopies):
-            total = total + zr[e - 1].astype(F32)
+            copy.wait_send()
+        for k in range(len(CHUNKS)):
+            for half in range(2):
+                slot = zr.at[2 * k + half]
+                landed = pltpu.make_async_remote_copy(
+                    src_ref=slot, dst_ref=slot, send_sem=zsend_sem.at[0],
+                    recv_sem=zrecv_sem.at[2 * k + half], device_id=at(dc=1), device_id_type=MESH,
+                )
+                if k:
+                    landed.wait_recv()
+                else:
+                    pl.when((zh != half) | (zh != c))(landed.wait_recv)
+        total = zr[0].astype(F32)
+        for slot in range(1, 16):
+            total = total + zr[slot].astype(F32)
         ig_buf[...] = total.astype(BF16)
         store(ig_buf, ig_out)
 
@@ -257,8 +288,11 @@
     )
     for name, *where in ORDER:
         steps[name](*where)
-    for copy in zcopies.values():
-        copy.wait_send()
+    for (k, f), copy in zcopies.items():
+        if k or f:
+            copy.wait_send()
+        else:
+            pl.when(zh != c)(copy.wait_send)
     for copy in stored:
         copy.wait()
 
@@ -311,9 +345,11 @@
             pltpu.VMEM((8, T, R), BF16),
             pltpu.VMEM((2 * HP, R), BF16),
             pltpu.VMEM((HP, R), BF16),
+            pltpu.VMEM((2 * HP, R), BF16),
             pltpu.VMEM((3 * HP, R), F32),
-            pltpu.VMEM((15, K, R), BF16),
-            pltpu.VMEM((2, K, R), F32),
+            pltpu.VMEM((16, K, R), BF16),
+            pltpu.SemaphoreType.DMA((16,)),
+            pltpu.SemaphoreType.DMA((16,)),
             pltpu.VMEM((K, R), BF16),
             pltpu.VMEM((3, H, R), BF16),
             pltpu.SemaphoreType.DMA((5,)),

time: 60.6 us -> 60.9 us (level)
  no operation moved by 1% of the time
where the time goes in v4:
time: 60.9 us; the launch traced here: 60.7 us
  Pallas kernels  60.1 us (99%)
  between operations  0.64 us (1%)
    pallas_call x1, Pallas kernels, body(): pl.pallas_call(kernel, out_shape=(jax.ShapeDtypeStruct((K, R), BF16), jax...  58.1 us
    pallas_call x1, Pallas kernels, body(): pl.pallas_call(land, out_shape=tuple((jax.ShapeDtypeStruct(p.shape, p.dty...  1.93 us

profile of v4, /device:TPU:1, one launch (start us, length us, event | category | flops | bytes accessed | tf_op | source)
XLA Modules:
  0.0 60.7 jit_solution(8486245097467088141)
XLA Ops:
  0.6 58.1 %swiglu_backward.1 = (bf16[16,512]{1,0:T(8,128)(2,1)}, bf16[224,512]{1,0:T(8,128)(2,1)}, bf16[224,512]{1,0:T(8,128)(2,1)}, bf16[224,512]{1,0:T(8,128)(2,1)}) custom-call(bf16[128,512]{1,0:T(8,128)(2,1)} %x_hbm.1, bf16[128,512]{1,0:T(8,128)(2,1)} %g_hbm.1, bf16[224,512]{1,0:T(8,128)(2,1)} %wg_hbm.1, bf16[224,512]{1,0:T(8,128)(2,1)} %wu_hbm.1, ...), custom_call_target="tpu_custom_call" | custom-call | tf_op jit(solution)/shard_map/swiglu_backward/pallas_call | solution.py:333
  58.8 1.9 %land.1 = (bf16[16,512]{1,0:T(8,128)(2,1)}, bf16[224,512]{1,0:T(8,128)(2,1)}, bf16[224,512]{1,0:T(8,128)(2,1)}, bf16[224,512]{1,0:T(8,128)(2,1)}) custom-call(bf16[16,512]{1,0:T(8,128)(2,1)} %get-tuple-element.8.refs_0_, bf16[224,512]{1,0:T(8,128)(2,1)} %get-tuple-element.9.refs_1_, bf16[224,512]{1,0:T(8,128)(2,1)} %get-tuple-element.10.refs_2_, ...), custom_call_target="tpu_custom_call" | custom-call | tf_op jit(solution)/shard_map/land/pallas_call | solution.py:368
